TPU v7x, 256 devices: a whole 4x4x8 slice. The times are simulated.
256 devices in a mesh: dp: 64 (over y_hi, z, x), tensor: 4 (over y_lo, core).
Axes of the slice: x: 4, y: 4 (y_hi: 2, y_lo: 2; y = y_hi * 2 + y_lo), z: 8, core: 2. Of those that a mesh axis runs over, the one named last changes fastest.
Arguments:
- activations: bfloat16 [16384, 8192], P('dp'), may hold values from -6 to 6
- out_grad: bfloat16 [16384, 22016], P('dp', 'tensor'), may hold values from -0.1875 to 0.1875
- basis: bfloat16 [8192, 512], P('dp', 'tensor'), may hold values from -0.0625 to 0.0625
- master: float32 [8192, 22016], P('dp', 'tensor'), may hold values from -4 to 4
- first_moment: float32 [512, 22016], P('dp', 'tensor'), may hold values from -6 to 6
- second_moment: float32 [512, 22016], P('dp', 'tensor'), may hold values from 0.01 to 0.25
Outputs:
- new_master: float32 [8192, 22016], P('dp', 'tensor')
- new_first: float32 [512, 22016], P('dp', 'tensor')
- new_second: float32 [512, 22016], P('dp', 'tensor')
All inputs are finite; a program needn't handle non-finite values.
Results may differ from a plain program's by a relative error of at most 0.00059.
Values may be sent and summed in bfloat16 or wider, within the bound.
A program may use at most 128 MiB of HBM per device.

v0:
```python
import math

import jax
import jax.numpy as jnp
from jax import lax
from jax.sharding import PartitionSpec as P

decay_first = 0.9
decay_second = 0.999
bias_first = 1.0 - math.exp(1000.0 * math.log(decay_first))
bias_second = 1.0 - math.exp(1000.0 * math.log(decay_second))
adam_eps = 1e-08
step_size = 0.025


def local(activations, out_grad, basis, master, first_moment, second_moment):
    rows_full = lax.all_gather(basis, "tensor", axis=1, tiled=True)
    projected = jnp.dot(
        activations,
        lax.all_gather(rows_full, "dp", axis=0, tiled=True),
        preferred_element_type=jnp.float32,
    ).astype(jnp.bfloat16)
    full_grad = lax.dot_general(
        projected, out_grad, (((0,), (0,)), ((), ())), preferred_element_type=jnp.float32
    )
    low_grad = lax.psum_scatter(full_grad, "dp", scatter_dimension=0, tiled=True)
    new_first = decay_first * first_moment + (1.0 - decay_first) * low_grad
    new_second = decay_second * second_moment + (1.0 - decay_second) * low_grad * low_grad
    factor = (new_first / bias_first / (jnp.sqrt(new_second / bias_second) + adam_eps)).astype(
        jnp.bfloat16
    )
    factor_all = lax.all_gather(factor, "dp", axis=0, tiled=True)
    expanded = jnp.dot(rows_full, factor_all, preferred_element_type=jnp.float32)
    new_master = master - step_size * expanded
    return (new_master, new_first, new_second)


def solution(mesh):
    placed = (
        P("dp", None),
        P("dp", "tensor"),
        P("dp", "tensor"),
        P("dp", "tensor"),
        P("dp", "tensor"),
        P("dp", "tensor"),
    )
    return jax.shard_map(
        local,
        mesh=mesh,
        in_specs=placed,
        out_specs=(P("dp", "tensor"), P("dp", "tensor"), P("dp", "tensor")),
        check_vma=False,
    )
```

profile of v0, /device:TPU:2, one launch (start us, length us, event | category | flops | bytes accessed | tf_op | source)
XLA Modules:
  0.0 1065.0 jit_solution(14023618339706433073)
XLA Ops:
  7.2 0.0 copy-start
  7.2 0.0 all-gather.3.cloned.1.call-start
  7.2 7.1 all_gather.9
  14.4 0.0 all-gather.3.cloned.1.call-update
  14.4 0.0 all-reduce.3.cloned.1.call-start
  14.4 149.9 %all-gather.3.cloned.1.call-done = bf16[8192,512]{1,0:T(8,128)(2,1)} async-done(((bf16[128,512]{1,0:T(8,128)(2,1)}), bf16[8192,512]{1,0:T(8,128)(2,1)}) %all-gather.3.cloned.1.call-update) | async-done | bytes 8388624 | tf_op jit(solution)/shard_map/all_gather | solution.py:20
  164.4 0.0 copy-done
  164.4 12.8 %fusion.2 = f32[512,5504]{1,0:T(8,128)} fusion(bf16[256,5504]{1,0:T(8,128)(2,1)S(1)} %copy-done, bf16[256,8192]{1,0:T(8,128)(2,1)} %param.6, bf16[8192,512]{1,0:T(8,128)(2,1)} %all-gather.3.cloned.1.call-done), kind=kOutput, calls=%fused_computation.4 | convolution fusion | flops 3590455296 | bytes 26673152 | tf_op jit(solution)/shard_map/dot_general | solution.py:23
  177.1 0.0 copy-start.4
  177.1 0.0 copy-start.2
  177.1 0.0 copy-start.3
  177.1 0.0 all-reduce.3.cloned.1.call-update
  177.2 0.0 copy-start.1
  177.2 0.0 all-gather.5.cloned.1.call-start
  177.2 0.6 copy-done.4
  177.8 0.6 dynamic-slice
  179.1 735.6 %all-reduce.3.cloned.1.call-done = f32[512,5504]{1,0:T(8,128)} async-done(((f32[512,5504]{1,0:T(8,128)}), f32[512,5504]{1,0:T(8,128)}) %all-reduce.3.cloned.1.call-update) | async-done | bytes 11272208
  914.6 0.0 copy-done.2
  914.6 0.0 copy-done.3
  914.6 1.7 divide_convert_fusion
  916.3 0.0 all-gather.5.cloned.1.call-update
  916.4 3.4 copy.11
  919.7 128.6 %all-gather.5.cloned.1.call-done = bf16[512,5504]{1,0:T(8,128)(2,1)} async-done(((bf16[8,5504]{1,0:T(8,128)(2,1)}), bf16[512,5504]{1,0:T(8,128)(2,1)}) %all-gather.5.cloned.1.call-update) | async-done | bytes 5636112 | tf_op jit(solution)/shard_map/all_gather | solution.py:32
  1048.4 0.0 copy-done.1
  1048.4 6.7 fusion.1
  1055.1 3.4 copy.12
Async XLA Ops:
  7.2 157.2 %copy-start = (bf16[256,5504]{1,0:T(8,128)(2,1)S(1)}, bf16[256,5504]{1,0:T(8,128)(2,1)}, u32[]{:S(2)}) copy-start(bf16[256,5504]{1,0:T(8,128)(2,1)} %param.7) | copy-start | bytes 8454148
  7.2 157.2 %all-gather.3.cloned.1.call-start = ((), (), s32[]{:S(2)}) async-start(), calls=%async_computation | async-start | bytes 8519680 | tf_op jit(solution)/shard_map/all_gather | solution.py:20
  14.4 900.2 %all-reduce.3.cloned.1.call-start = ((), (), s32[]{:S(2)}) async-start(), calls=%async_computation.2 | async-start | bytes 22544384
  177.1 0.7 copy-start.4
  177.1 737.5 %copy-start.2 = (f32[8,5504]{1,0:T(8,128)S(1)}, f32[8,5504]{1,0:T(8,128)}, u32[]{:S(2)}) copy-start(f32[8,5504]{1,0:T(8,128)} %param.11) | copy-start | bytes 528388
  177.1 737.5 %copy-start.3 = (f32[8,5504]{1,0:T(8,128)S(1)}, f32[8,5504]{1,0:T(8,128)}, u32[]{:S(2)}) copy-start(f32[8,5504]{1,0:T(8,128)} %param.10) | copy-start | bytes 528388
  177.2 871.2 %copy-start.1 = (bf16[128,512]{1,0:T(8,128)(2,1)S(1)}, bf16[128,512]{1,0:T(8,128)(2,1)}, u32[]{:S(2)}) copy-start(bf16[128,512]{1,0:T(8,128)(2,1)} %all_gather.9) | copy-start | bytes 393220
  177.2 871.2 %all-gather.5.cloned.1.call-start = ((), (), s32[]{:S(2)}) async-start(), calls=%async_computation.1 | async-start | bytes 5724160 | tf_op jit(solution)/shard_map/all_gather | solution.py:32
Sparse Core Ops, SparseCore 0:
  14.5 149.8 all-gather.2
  177.3 737.2 all-reduce.2
  918.2 130.1 all-gather.4
where the time goes:
time: 1070 us; the launch traced here: 1060 us
  waiting for transfers between devices  1010 us (94%)
  matrix products  19.5 us (2%)
  between operations  14.4 us (1%)
    unnamed x4, waiting for transfers between devices  736 us
    all_gather x1, waiting for transfers between devices, local(): lax.all_gather(rows_full, 'dp', axis=0, tiled=True)  150 us
    all_gather x1, waiting for transfers between devices, local(): factor_all = lax.all_gather(factor, 'dp', axis=0, tiled=True)  129 us
  transfers between devices with their start and end apart: 3, of which 3 were waited for; matrix products, arithmetic and copies ran while one was open for 0% of the time, Pallas kernels for 0%

commit v1 on v0

v1 whole, which is shorter than its diff:
```python
import math

import jax
import jax.numpy as jnp
from jax import lax
from jax.experimental import pallas as pl
from jax.experimental.pallas import tpu as pltpu
from jax.sharding import PartitionSpec as P

MESH = pl.DeviceIdType.MESH
F32 = jnp.float32
BF16 = jnp.bfloat16

decay_first = 0.9
decay_second = 0.999
bias_first = 1.0 - math.exp(1000.0 * math.log(decay_first))
bias_second = 1.0 - math.exp(1000.0 * math.log(decay_second))
adam_eps = 1e-08
step_size = 0.025

NX, NZ, NG = 4, 8, 8
W = 768
TOP = 5504 // 128 - W // 128
CW = 384
NC = W // CW


def kernel(
    act_h, og_h, bas_h, mas_h, fm_h, sm_h,
    om, of, os_,
    act, og, bas, mas, projt, part, rsr, mom, sec, nfr, nsr, fac, lhs, exs, exr,
    lsem, bs, br, zs, zr, gs, gr, ms, mr, ps, pr, ys, yr, cs, cr,
    ts, tr, rs, rr, fs, fr, es, er, ns, nr,
):
    d = lax.axis_index("dp")
    t = lax.axis_index("tensor")
    x = lax.rem(d, 4)
    z = lax.rem(d // 4, 8)
    yh = d // 32
    g = yh * 4 + x

    def dev(yy, zz, xx):
        return yy * 32 + zz * 4 + xx

    def wrapz(v):
        return lax.rem(v + 16, 8)

    def member(j, sign):
        yy = lax.rem(yh + j // 4, 2)
        xx = lax.rem(x + sign * (j % 4) + 4, 4)
        return yy, xx

    def start_of(k):
        return pl.multiple_of(jnp.minimum(k * (W // 128), TOP) * 128, 128)

    def rcopy(src, dst, s, r, to):
        return pltpu.make_async_remote_copy(
            src_ref=src, dst_ref=dst, send_sem=s, recv_sem=r, device_id=to, device_id_type=MESH
        )

    t1 = t + 1 - 2 * lax.rem(t, 2)
    t2 = lax.rem(t + 2, 4)
    t3 = lax.rem(t1 + 2, 4)
    up, down = (dev(yh, wrapz(z + 1), x), t), (dev(yh, wrapz(z - 1), x), t)
    dy = dev(1 - yh, z, x)
    group = []
    for j in range(1, NG):
        yy, xx = member(j, 1)
        group.append((dev(yy, z, xx), t))
    partners = group + [up, down, (d, t1), (d, t2), (d, t3), (dy, t2)]

    loads = [
        pltpu.make_async_copy(act_h, act, lsem.at[0]),
        pltpu.make_async_copy(mas_h, mas, lsem.at[1]),
        pltpu.make_async_copy(og_h.at[:, pl.ds(start_of(g), W)], og.at[g], lsem.at[2]),
        pltpu.make_async_copy(bas_h, bas.at[z, g], lsem.at[3]),
        pltpu.make_async_copy(
            fm_h.at[:, pl.ds(start_of(g), W)], mom.at[pl.ds(pl.multiple_of(g * 8, 8), 8)], lsem.at[4]
        ),
        pltpu.make_async_copy(
            sm_h.at[:, pl.ds(start_of(g), W)], sec.at[pl.ds(pl.multiple_of(g * 8, 8), 8)], lsem.at[5]
        ),
    ]
    for c in loads:
        c.start()

    barrier = pltpu.get_barrier_semaphore()
    for p in partners:
        pl.semaphore_signal(barrier, inc=1, device_id=p, device_id_type=MESH)
    pl.semaphore_wait(barrier, len(partners))

    sends = []

    def go(c):
        c.start()
        sends.append(c)
        return c

    b_in = [go(rcopy(bas_h, bas.at[z, g], bs.at[j], br.at[j], group[j - 1])) for j in range(1, NG)]
    m_in, g_in = [], []
    for j in range(1, NG):
        yy, xx = member(j, 1)
        k = yy * 4 + xx
        rows = pl.ds(pl.multiple_of(g * 8, 8), 8)
        to = group[j - 1]
        g_in.append(go(rcopy(og_h.at[:, pl.ds(start_of(k), W)], og.at[g], gs.at[j], gr.at[j], to)))
    for j in range(1, NG):
        yy, xx = member(j, 1)
        k = yy * 4 + xx
        rows = pl.ds(pl.multiple_of(g * 8, 8), 8)
        to = group[j - 1]
        m_in.append(go(rcopy(fm_h.at[:, pl.ds(start_of(k), W)], mom.at[rows], ms.at[0, j], mr.at[0, j], to)))
        m_in.append(go(rcopy(sm_h.at[:, pl.ds(start_of(k), W)], sec.at[rows], ms.at[1, j], mr.at[1, j], to)))
    for c in b_in:
        c.wait_recv()
    loads[3].wait()

    def zsend(way, s, h):
        zz = wrapz(z - s) if way == 0 else wrapz(z + s)
        blk = bas.at[zz, pl.ds(h * 4, 4)]
        return go(rcopy(blk, blk, zs.at[way, s, h], zr.at[way, s, h], up if way == 0 else down))

    def hops(s):
        return [(w, h) for h in (0, 1) for w in (0, 1) if s < 3 or w == h]

    def project(zz, h):
        cols = pl.ds(pl.multiple_of((h * 32 + zz * 4) * 128, 512), 512)
        return jnp.dot(
            act[:, cols], bas[zz, h * 4 : h * 4 + 4].reshape(512, 128), preferred_element_type=F32
        )

    moving = {(0, w, h): zsend(w, 0, h) for w, h in hops(0)}
    t_in = []
    own = pl.ds(pl.multiple_of(t * 128, 128), 128)
    for i, q in enumerate((t1, t2, t3)):
        t_in.append(go(rcopy(bas.at[z], lhs.at[:, :, own], ts.at[i], tr.at[i], (d, q))))
    lhs[:, :, own] = bas[z]
    loads[0].wait()
    total = project(z, 0) + project(z, 1)
    for s in range(4):
        for w, h in hops(s):
            moving[(s, w, h)].wait_recv()
            if s < 3 and (w, h) in hops(s + 1):
                moving[(s + 1, w, h)] = zsend(w, s + 1, h)
        for w, h in hops(s):
            total = total + project(wrapz(z - s - 1) if w == 0 else wrapz(z + s + 1), h)

    rows_t = pl.ds(pl.multiple_of(t * 128, 128), 128)
    rows_u = pl.ds(pl.multiple_of(t2 * 128, 128), 128)
    cols_g = pl.ds(pl.multiple_of(g * 256, 256), 256)
    projt[rows_t, cols_g] = total.T.astype(BF16)
    p_in = []
    for j in range(1, NX):
        blk = projt.at[rows_t, cols_g]
        p_in.append(go(rcopy(blk, blk, ps.at[j], pr.at[j], group[j - 1])))
    for c in p_in:
        c.wait_recv()
    half = lambda yy: pl.ds(pl.multiple_of(yy * 1024, 1024), 1024)
    blk = projt.at[rows_t, half(yh)]
    y_in = [
        go(rcopy(blk, blk, ys.at[i], yr.at[i], to)) for i, to in enumerate([(d, t2), (dy, t2), (dy, t)])
    ]
    c_in = [go(rcopy(blk, blk, cs.at[3], cr.at[3], (d, t1)))]
    for i, (rows, yy) in enumerate([(rows_u, yh), (rows_u, 1 - yh), (rows_t, 1 - yh)]):
        y_in[i].wait_recv()
        blk = projt.at[rows, half(yy)]
        c_in.append(go(rcopy(blk, blk, cs.at[i], cr.at[i], (d, t1))))
    loads[2].wait()
    for c in g_in:
        c.wait_recv()
    for c in c_in:
        c.wait_recv()

    def multiply(i, carry):
        cols = pl.ds(pl.multiple_of(i * 256, 256), 256)
        part[:, cols] = jnp.dot(
            projt[...], og[:, :, cols].reshape(2048, 256), preferred_element_type=F32
        )
        return carry

    lax.fori_loop(0, W // 256, multiply, 0)

    def rows_of(w, b):
        return pl.ds(pl.multiple_of(w * 256 + b * 32, 32), 32)

    def rsend(w, c, s):
        b = wrapz(z - 1 - s) if w == 0 else wrapz(z + 1 + s)
        src = part.at[rows_of(w, b), pl.ds(c * CW, CW)]
        return go(rcopy(src, rsr.at[w, c, s], rs.at[w, c, s], rr.at[w, c, s], up if w == 0 else down))

    moving = {(w, c): rsend(w, c, 0) for c in range(NC) for w in (0, 1)}
    for s in range(7):
        for c in range(NC):
            for w in (0, 1):
                moving[(w, c)].wait_recv()
                b = wrapz(z - 2 - s) if w == 0 else wrapz(z + 2 + s)
                cols = pl.ds(c * CW, CW)
                part[rows_of(w, b), cols] = part[rows_of(w, b), cols] + rsr[w, c, s]
                if s < 6:
                    moving[(w, c)] = rsend(w, c, s + 1)

    loads[4].wait()
    loads[5].wait()
    for c in m_in:
        c.wait_recv()
    for w in (0, 1):
        rows = slice(w * 32, w * 32 + 32)
        grad = part[rows_of(w, z), :]
        first = decay_first * mom[rows] + (1.0 - decay_first) * grad
        second = decay_second * sec[rows] + (1.0 - decay_second) * grad * grad
        mom[rows] = first
        sec[rows] = second
        fac[w, z] = (
            first / bias_first / (jnp.sqrt(second / bias_second) + adam_eps)
        ).astype(BF16)

    def fsend(way, s, h):
        zz = wrapz(z - s) if way == 0 else wrapz(z + s)
        blk = fac.at[h, zz]
        return go(rcopy(blk, blk, fs.at[way, s, h], fr.at[way, s, h], up if way == 0 else down))

    moving = {(0, w, h): fsend(w, 0, h) for w, h in hops(0)}
    n_in = []
    for j in range(1, NG):
        yy, xx = member(j, 1)
        k = yy * 4 + xx
        rows = pl.ds(pl.multiple_of(k * 8, 8), 8)
        to = group[j - 1]
        n_in.append(go(rcopy(mom.at[rows], nfr.at[g], ns.at[0, j], nr.at[0, j], to)))
        n_in.append(go(rcopy(sec.at[rows], nsr.at[g], ns.at[1, j], nr.at[1, j], to)))
    mine = pl.ds(pl.multiple_of(g * 8, 8), 8)
    nfr[g] = mom[mine]
    nsr[g] = sec[mine]
    for s in range(4):
        for w, h in hops(s):
            moving[(s, w, h)].wait_recv()
            if s < 3 and (w, h) in hops(s + 1):
                moving[(s + 1, w, h)] = fsend(w, s + 1, h)

    for c in t_in:
        c.wait_recv()
    e_in = []
    for j in (6, 2, 5, 7, 4, 1, 3, 0):
        yy, xx = member(j, 1)
        k = yy * 4 + xx
        res = jnp.dot(lhs[k], fac[...].reshape(512, W), preferred_element_type=F32)
        if j == 0:
            exr[g] = res
        else:
            exs[j] = res
            e_in.append((j, go(rcopy(exs.at[j], exr.at[g], es.at[j], er.at[j], group[j - 1]))))

    for c in n_in:
        c.wait_recv()
    loads[1].wait()
    for k in range(NG):
        at = min(k * (W // 128), TOP) * 128
        of[:, at : at + W] = nfr[k]
        os_[:, at : at + W] = nsr[k]

    def finish(k):
        cols = pl.ds(start_of(k), W)
        om[:, cols] = mas[:, cols] - step_size * exr[k]

    finish(g)
    for j, c in e_in:
        c.wait_recv()
        yy, xx = member(j, -1)
        finish(yy * 4 + xx)
    for c in sends:
        c.wait_send()


def local(activations, out_grad, basis, master, first_moment, second_moment):
    dma = pltpu.SemaphoreType.DMA
    sems = [
        dma((6,)),
        dma((8,)), dma((8,)),
        dma((2, 4, 2)), dma((2, 4, 2)),
        dma((8,)), dma((8,)),
        dma((2, 8)), dma((2, 8)),
        dma((4,)), dma((4,)),
        dma((3,)), dma((3,)),
        dma((4,)), dma((4,)),
        dma((3,)), dma((3,)),
        dma((2, NC, 7)), dma((2, NC, 7)),
        dma((2, 4, 2)), dma((2, 4, 2)),
        dma((8,)), dma((8,)),
        dma((2, 8)), dma((2, 8)),
    ]
    return pl.pallas_call(
        kernel,
        out_shape=(
            jax.ShapeDtypeStruct((128, 5504), F32),
            jax.ShapeDtypeStruct((8, 5504), F32),
            jax.ShapeDtypeStruct((8, 5504), F32),
        ),
        in_specs=[pl.BlockSpec(memory_space=pl.ANY)] * 6,
        out_specs=[pl.BlockSpec(memory_space=pltpu.VMEM)] * 3,
        scratch_shapes=[
            pltpu.VMEM((256, 8192), BF16),
            pltpu.VMEM((NG, 256, W), BF16),
            pltpu.VMEM((NZ, NG, 128, 128), BF16),
            pltpu.VMEM((128, 5504), F32),
            pltpu.VMEM((512, 2048), BF16),
            pltpu.VMEM((512, W), F32),
            pltpu.VMEM((2, NC, 7, 32, CW), F32),
            pltpu.VMEM((64, W), F32),
            pltpu.VMEM((64, W), F32),
            pltpu.VMEM((NG, 8, W), F32),
            pltpu.VMEM((NG, 8, W), F32),
            pltpu.VMEM((2, NZ, 32, W), BF16),
            pltpu.VMEM((NG, 128, 512), BF16),
            pltpu.VMEM((NG, 128, W), F32),
            pltpu.VMEM((NG, 128, W), F32),
        ]
        + sems,
        compiler_params=pltpu.CompilerParams(
            collective_id=0, has_side_effects=True, vmem_limit_bytes=56 << 20
        ),
    )(activations, out_grad, basis, master, first_moment, second_moment)


def solution(mesh):
    placed = (
        P("dp", None),
        P("dp", "tensor"),
        P("dp", "tensor"),
        P("dp", "tensor"),
        P("dp", "tensor"),
        P("dp", "tensor"),
    )
    return jax.shard_map(
        local,
        mesh=mesh,
        in_specs=placed,
        out_specs=(P("dp", "tensor"), P("dp", "tensor"), P("dp", "tensor")),
        check_vma=False,
    )
```

time: 1070 us -> 167 us (0.16)
  the two profiles are of different devices: /device:TPU:2 before, /device:TPU:38 now
where the time goes in v1:
time: 167 us
  Pallas kernels  161 us (96%)
  local copies, waits for them, and re-layouts  4.93 us (3%)
    pallas_call x1, Pallas kernels, local(): pl.pallas_call(kernel, out_shape=(jax.ShapeDtypeStruct((128, 5504), F32),...  161 us
    unnamed x7, local copies, waits for them, and re-layouts  4.93 us

profile of v1, /device:TPU:38, one launch (start us, length us, event | category | flops | bytes accessed | tf_op | source)
XLA Modules:
  0.0 166.8 jit_solution(16104550666220321348)
XLA Ops:
  0.6 161.2 %shard_map.85 = (f32[128,5504]{1,0:T(8,128)}, f32[8,5504]{1,0:T(8,128)}, f32[8,5504]{1,0:T(8,128)}) custom-call(bf16[256,8192]{1,0:T(8,128)(2,1)} %act_h.1, bf16[256,5504]{1,0:T(8,128)(2,1)} %og_h.1, bf16[128,128]{1,0:T(8,128)(2,1)} %bas_h.1, f32[128,5504]{1,0:T(8,128)} %mas_h.1, f32[8,5504]{1,0:T(8,128)} %fm_h.1, f32[8,5504]{1,0:T(8,128)} %sm_h.1), custom_call_target="tpu_custom_call" | custom-call | tf_op jit(solution)/shard_map/pallas_call | solution.py:291
  161.8 0.0 copy-start.1
  161.8 0.0 copy-start
  161.8 3.6 %copy.12 = f32[128,5504]{1,0:T(8,128)} copy(f32[128,5504]{1,0:T(8,128)} %get-tuple-element.6) | data formatting | bytes 5636096
  165.4 0.0 copy-done.1
  165.4 0.7 copy.13
  166.1 0.0 copy-done
  166.1 0.7 copy.14
Async XLA Ops:
  161.8 3.6 %copy-start.1 = (f32[8,5504]{1,0:T(8,128)S(1)}, f32[8,5504]{1,0:T(8,128)}, u32[]{:S(2)}) copy-start(f32[8,5504]{1,0:T(8,128)} %get-tuple-element.7) | copy-start | bytes 528388
  161.8 4.3 %copy-start = (f32[8,5504]{1,0:T(8,128)S(1)}, f32[8,5504]{1,0:T(8,128)}, u32[]{:S(2)}) copy-start(f32[8,5504]{1,0:T(8,128)} %get-tuple-element.8) | copy-start | bytes 528388

commit v2 on v0

v2 whole, which is shorter than its diff:
```python
import math

import jax
import jax.numpy as jnp
from jax import lax
from jax.experimental import pallas as pl
from jax.experimental.pallas import tpu as pltpu
from jax.sharding import PartitionSpec as P

MESH = pl.DeviceIdType.MESH
F32 = jnp.float32
BF16 = jnp.bfloat16

decay_first = 0.9
decay_second = 0.999
bias_first = 1.0 - math.exp(1000.0 * math.log(decay_first))
bias_second = 1.0 - math.exp(1000.0 * math.log(decay_second))
adam_eps = 1e-08
step_size = 0.025

NX, NZ, NG = 4, 8, 8
W = 768
TOP = 5504 // 128 - W // 128
CW = 256
NC = W // CW
ORDER = (6, 2, 5, 7, 4, 1, 3)


def kernel(
    act_h, og_h, bas_h, mas_h, fm_h, sm_h,
    om, of, os_,
    act, og, bas, mas, projt, part, rsr, mom, sec, nfr, nsr, fac, home, lhs, exs, exr,
    lsem, bs, br, zs, zr, gs, gr, ms, mr, p1s, p1r, p2s, p2r, cs, cr,
    ts, tr, rs, rr, fs, fr, qs, qr, us, ur, es, er, ns, nr,
):
    d = lax.axis_index("dp")
    t = lax.axis_index("tensor")
    x = lax.rem(d, 4)
    z = lax.rem(d // 4, 8)
    yh = d // 32
    g = yh * 4 + x

    def dev(yy, zz, xx):
        return yy * 32 + zz * 4 + xx

    def wrapz(v):
        return lax.rem(v + 16, 8)

    def member(j, sign):
        yy = lax.rem(yh + j // 4, 2)
        xx = lax.rem(x + sign * (j % 4) + 4, 4)
        return yy, xx

    def index(j, sign):
        yy, xx = member(j, sign)
        return yy * 4 + xx

    def start_of(k):
        return pl.multiple_of(jnp.minimum(k * (W // 128), TOP) * 128, 128)

    def span(first, size):
        return pl.ds(pl.multiple_of(first, size), size)

    def rcopy(src, dst, s, r, to):
        return pltpu.make_async_remote_copy(
            src_ref=src, dst_ref=dst, send_sem=s, recv_sem=r, device_id=to, device_id_type=MESH
        )

    t1 = t + 1 - 2 * lax.rem(t, 2)
    t2 = lax.rem(t + 2, 4)
    ring = ((dev(yh, wrapz(z + 1), x), t), (dev(yh, wrapz(z - 1), x), t))
    dy = dev(1 - yh, z, x)
    group = [None]
    for j in range(1, NG):
        yy, xx = member(j, 1)
        group.append((dev(yy, z, xx), t))
    core = (d, t1)
    yside = ((d, t2), (dy, t2), (dy, t))
    partners = group[1:] + [ring[0], ring[1], core, (d, t2), (dy, t2)]

    eight = span(g * 8, 8)
    loads = [
        pltpu.make_async_copy(bas_h, bas.at[z, g], lsem.at[3]),
        pltpu.make_async_copy(act_h, act, lsem.at[0]),
        pltpu.make_async_copy(mas_h, mas, lsem.at[1]),
        pltpu.make_async_copy(og_h.at[:, pl.ds(start_of(g), W)], og.at[g], lsem.at[2]),
        pltpu.make_async_copy(fm_h.at[:, pl.ds(start_of(g), W)], mom.at[eight], lsem.at[4]),
        pltpu.make_async_copy(sm_h.at[:, pl.ds(start_of(g), W)], sec.at[eight], lsem.at[5]),
    ]
    for c in loads:
        c.start()

    barrier = pltpu.get_barrier_semaphore()
    for p in partners:
        pl.semaphore_signal(barrier, inc=1, device_id=p, device_id_type=MESH)
    pl.semaphore_wait(barrier, len(partners))

    sends = []

    def go(c):
        c.start()
        sends.append(c)
        return c

    b_in = [go(rcopy(bas_h, bas.at[z, g], bs.at[j], br.at[j], group[j])) for j in ORDER]
    for c in b_in:
        c.wait_recv()
    loads[0].wait()

    def hops(s):
        return [(w, h) for h in (0, 1) for w in (0, 1) if s < 3 or w == h]

    def gather(block, send, recv):
        moving = {}

        def send_step(s):
            for w, h in hops(s):
                if s > 0:
                    moving[(s - 1, w, h)].wait_recv()
                zz = wrapz(z - s) if w == 0 else wrapz(z + s)
                blk = block(zz, h)
                moving[(s, w, h)] = go(rcopy(blk, blk, send.at[w, s, h], recv.at[w, s, h], ring[w]))

        def last():
            for s in (2, 3):
                for w, h in hops(s):
                    if (s, w, h) in moving and not (s == 2 and (w, h) in hops(3)):
                        moving[(s, w, h)].wait_recv()

        return send_step, last

    def project(zz, h):
        return jnp.dot(
            act[:, span((h * 32 + zz * 4) * 128, 512)],
            bas[zz, h * 4 : h * 4 + 4].reshape(512, 128),
            preferred_element_type=F32,
        )

    step, last = gather(lambda zz, h: bas.at[zz, pl.ds(h * 4, 4)], zs, zr)
    step(0)

    def grad_send(i, first, size):
        return [
            go(
                rcopy(
                    og_h.at[:, pl.ds(pl.multiple_of(start_of(index(j, 1)) + first, 128), size)],
                    og.at[g, :, pl.ds(first, size)],
                    gs.at[i, j],
                    gr.at[i, j],
                    group[j],
                )
            )
            for j in ORDER
        ]

    g_in = [grad_send(0, 0, 512)]
    rows_t, rows_u = span(t * 128, 128), span(t2 * 128, 128)
    t_in = [go(rcopy(bas.at[z], lhs.at[:, :, rows_t], ts.at[0], tr.at[0], core))]
    lhs[:, :, rows_t] = bas[z]
    loads[1].wait()
    total = project(z, 0) + project(z, 1)
    for s in range(1, 4):
        step(s)
        for w, h in hops(s - 1):
            if s < 3 or (w, h) in hops(3):
                total = total + project(wrapz(z - s) if w == 0 else wrapz(z + s), h)
    last()
    for w, h in hops(2):
        if (w, h) not in hops(3):
            total = total + project(wrapz(z - 3) if w == 0 else wrapz(z + 3), h)
    for w, h in hops(3):
        total = total + project(wrapz(z - 4), h)

    top_t, low_t = span(t * 128, 64), pl.ds(pl.multiple_of(t * 128 + 64, 64), 64)
    top_u, low_u = span(t2 * 128, 64), pl.ds(pl.multiple_of(t2 * 128 + 64, 64), 64)
    cols_x = span(x * 256, 256)
    projt[yh, rows_t, cols_x] = total.T.astype(BF16)
    blk = projt.at[yh, top_t, cols_x]
    xa = [go(rcopy(blk, blk, p1s.at[j], p1r.at[j], group[j])) for j in (2, 1, 3)]
    blk = projt.at[yh, low_t, cols_x]
    yb = [go(rcopy(blk, blk, p1s.at[4 + i], p1r.at[4 + i], to)) for i, to in enumerate(yside)]
    for c in xa:
        c.wait_recv()
    blk = projt.at[yh, top_t]
    ya = [go(rcopy(blk, blk, p2s.at[i], p2r.at[i], to)) for i, to in enumerate(yside)]
    for c in yb:
        c.wait_recv()
    xb = []
    for i, rows in enumerate((low_t, low_u)):
        blk = projt.at[:, rows, cols_x]
        xb += [go(rcopy(blk, blk, p2s.at[4 * i + 3 + j], p2r.at[4 * i + 3 + j], group[j])) for j in (2, 1, 3)]
    blk = projt.at[yh, top_t]
    c_in = [go(rcopy(blk, blk, cs.at[0], cr.at[0], core))]
    for i, (rows, yy) in enumerate([(top_u, yh), (top_u, 1 - yh), (top_t, 1 - yh)]):
        ya[i].wait_recv()
        blk = projt.at[yy, rows]
        c_in.append(go(rcopy(blk, blk, cs.at[i + 1], cr.at[i + 1], core)))
    for i, rows in enumerate((low_t, low_u)):
        for c in xb[3 * i : 3 * i + 3]:
            c.wait_recv()
        blk = projt.at[:, rows]
        c_in.append(go(rcopy(blk, blk, cs.at[i + 4], cr.at[i + 4], core)))
    for c in c_in:
        c.wait_recv()
    loads[3].wait()
    for c in g_in[0]:
        c.wait_recv()

    def multiply(c):
        cols = slice(c * CW, c * CW + CW)
        part[:, cols] = jnp.dot(
            projt[0], og[0:4, :, cols].reshape(1024, CW), preferred_element_type=F32
        ) + jnp.dot(projt[1], og[4:8, :, cols].reshape(1024, CW), preferred_element_type=F32)

    def rows_of(w, b):
        return pl.ds(pl.multiple_of(w * 256 + b * 32, 32), 32)

    def rsend(w, h, c, s):
        b = wrapz(z + 4 - s) if w == 0 else wrapz(z - 4 + s)
        src = part.at[rows_of(h, b), pl.ds(c * CW, CW)]
        return go(rcopy(src, rsr.at[w, h, c, s], rs.at[w, h, c, s], rr.at[w, h, c, s], ring[w]))

    moving = {}

    def begin(c):
        multiply(c)
        for w, h in ((0, 0), (1, 1), (0, 1), (1, 0)):
            moving[(w, h, c)] = rsend(w, h, c, 0 if w == h else 1)

    def reduce(c, s):
        for w, h in ((0, 0), (1, 1), (0, 1), (1, 0)):
            if s == 0 and w != h:
                continue
            moving[(w, h, c)].wait_recv()
            b = wrapz(z + 3 - s) if w == 0 else wrapz(z - 3 + s)
            cols = pl.ds(c * CW, CW)
            part[rows_of(h, b), cols] = part[rows_of(h, b), cols] + rsr[w, h, c, s]
            if s < 3:
                moving[(w, h, c)] = rsend(w, h, c, s + 1)

    def adam(c, put):
        cols = slice(c * CW, c * CW + CW)
        for w in (0, 1):
            rows = slice(w * 32, w * 32 + 32)
            grad = part[rows_of(w, z), cols]
            first = decay_first * mom[rows, cols] + (1.0 - decay_first) * grad
            second = decay_second * sec[rows, cols] + (1.0 - decay_second) * grad * grad
            mom[rows, cols] = first
            sec[rows, cols] = second
            put(w, (first / bias_first / (jnp.sqrt(second / bias_second) + adam_eps)).astype(BF16))

    def put_home(w, v):
        home[g, w, z] = v

    def put_fac(c):
        def put(w, v):
            fac[c - 1, w, z] = v

        return put

    begin(1)
    begin(0)
    m_in = []
    for j in ORDER:
        cols = pl.ds(start_of(index(j, 1)), W)
        m_in.append(go(rcopy(fm_h.at[:, cols], mom.at[eight], ms.at[0, j], mr.at[0, j], group[j])))
        m_in.append(go(rcopy(sm_h.at[:, cols], sec.at[eight], ms.at[1, j], mr.at[1, j], group[j])))
    g_in.append(grad_send(1, 512, 256))
    t_in.append(go(rcopy(bas.at[z], lhs.at[:, :, rows_t], ts.at[1], tr.at[1], (d, t2))))
    for s in range(4):
        reduce(1, s)
        reduce(0, s)
    loads[4].wait()
    loads[5].wait()
    for c in m_in:
        c.wait_recv()
    step1, last1 = gather(lambda zz, h: fac.at[0, h, zz], fs.at[0], fr.at[0])
    step2, last2 = gather(lambda zz, h: fac.at[1, h, zz], fs.at[1], fr.at[1])
    step0, last0 = gather(lambda zz, h: home.at[:, h, zz], us, ur)
    adam(1, put_fac(1))
    step1(0)
    adam(0, put_home)
    blk = home.at[g, :, z]
    q_in = [go(rcopy(blk, blk, qs.at[j], qr.at[j], group[j])) for j in ORDER]
    for c in g_in[1]:
        c.wait_recv()
    begin(2)
    step1(1)
    reduce(2, 0)
    step1(2)
    reduce(2, 1)
    step1(3)
    reduce(2, 2)
    t_in[1].wait_recv()
    blk = lhs.at[:, :, rows_u]
    t_in.append(go(rcopy(blk, blk, ts.at[2], tr.at[2], core)))
    last1()

    e_in = {}

    def expand(c):
        for j in ORDER + (0,):
            res = jnp.dot(lhs[index(j, 1)], fac[c - 1].reshape(512, CW), preferred_element_type=F32)
            cols = slice((c - 1) * CW, c * CW)
            if j == 0:
                exr[g, :, cols] = res
            else:
                exs[j, :, cols] = res
                e_in[(c, j)] = go(
                    rcopy(
                        exs.at[j, :, cols],
                        exr.at[g, :, cols],
                        es.at[c - 1, j],
                        er.at[c - 1, j],
                        group[j],
                    )
                )

    for c in t_in:
        if c is not t_in[1]:
            c.wait_recv()
    expand(1)
    reduce(2, 3)
    adam(2, put_fac(2))
    step2(0)
    for c in q_in:
        c.wait_recv()
    step0(0)
    n_in = []
    for j in ORDER:
        rows = span(index(j, 1) * 8, 8)
        n_in.append(go(rcopy(mom.at[rows], nfr.at[g], ns.at[0, j], nr.at[0, j], group[j])))
        n_in.append(go(rcopy(sec.at[rows], nsr.at[g], ns.at[1, j], nr.at[1, j], group[j])))
    nfr[g] = mom[eight]
    nsr[g] = sec[eight]
    step2(1)
    step2(2)
    step2(3)
    step0(1)
    last2()
    expand(2)
    for c in n_in:
        c.wait_recv()
    for k in range(NG):
        at = min(k * (W // 128), TOP) * 128
        of[:, at : at + W] = nfr[k]
        os_[:, at : at + W] = nsr[k]
    loads[2].wait()
    step0(2)
    step0(3)
    last0()
    for k in range(NG):
        at = min(k * (W // 128), TOP) * 128
        res = jnp.dot(lhs[g], home[k].reshape(512, CW), preferred_element_type=F32)
        om[:, at : at + CW] = mas[:, at : at + CW] - step_size * res

    def finish(k):
        cols = pl.ds(pl.multiple_of(start_of(k) + CW, 128), W - CW)
        om[:, cols] = mas[:, cols] - step_size * exr[k]

    finish(g)
    for j in ORDER:
        e_in[(1, j)].wait_recv()
        e_in[(2, j)].wait_recv()
        finish(index(j, -1))
    for c in sends:
        c.wait_send()


def local(activations, out_grad, basis, master, first_moment, second_moment):
    dma = pltpu.SemaphoreType.DMA
    sems = [dma((6,))]
    for shape in (
        (8,),
        (2, 4, 2),
        (2, 8),
        (2, 8),
        (8,),
        (12,),
        (6,),
        (3,),
        (2, 2, NC, 4),
        (2, 2, 4, 2),
        (8,),
        (2, 4, 2),
        (2, 8),
        (2, 8),
    ):
        sems += [dma(shape), dma(shape)]
    return pl.pallas_call(
        kernel,
        out_shape=(
            jax.ShapeDtypeStruct((128, 5504), F32),
            jax.ShapeDtypeStruct((8, 5504), F32),
            jax.ShapeDtypeStruct((8, 5504), F32),
        ),
        in_specs=[pl.BlockSpec(memory_space=pl.ANY)] * 6,
        out_specs=[pl.BlockSpec(memory_space=pltpu.VMEM)] * 3,
        scratch_shapes=[
            pltpu.VMEM((256, 8192), BF16),
            pltpu.VMEM((NG, 256, W), BF16),
            pltpu.VMEM((NZ, NG, 128, 128), BF16),
            pltpu.VMEM((128, 5504), F32),
            pltpu.VMEM((2, 512, 1024), BF16),
            pltpu.VMEM((512, W), F32),
            pltpu.VMEM((2, 2, NC, 4, 32, CW), F32),
            pltpu.VMEM((64, W), F32),
            pltpu.VMEM((64, W), F32),
            pltpu.VMEM((NG, 8, W), F32),
            pltpu.VMEM((NG, 8, W), F32),
            pltpu.VMEM((2, 2, NZ, 32, CW), BF16),
            pltpu.VMEM((NG, 2, NZ, 32, CW), BF16),
            pltpu.VMEM((NG, 128, 512), BF16),
            pltpu.VMEM((NG, 128, W - CW), F32),
            pltpu.VMEM((NG, 128, W - CW), F32),
        ]
        + sems,
        compiler_params=pltpu.CompilerParams(
            collective_id=0, has_side_effects=True, vmem_limit_bytes=56 << 20
        ),
    )(activations, out_grad, basis, master, first_moment, second_moment)


def solution(mesh):
    placed = (
        P("dp", None),
        P("dp", "tensor"),
        P("dp", "tensor"),
        P("dp", "tensor"),
        P("dp", "tensor"),
        P("dp", "tensor"),
    )
    return jax.shard_map(
        local,
        mesh=mesh,
        in_specs=placed,
        out_specs=(P("dp", "tensor"), P("dp", "tensor"), P("dp", "tensor")),
        check_vma=False,
    )
```

time: 1070 us -> 132 us (0.12)
  waiting for transfers between devices: 1010 us -> 0 us
  Pallas kernels: 0 us -> 127 us
  matrix products: 19.5 us -> 0 us
  between operations: 14.4 us -> 0.66 us
    unnamed x4 -> x0, waiting for transfers between devices: 736 us -> none
    all_gather x2 -> x0, waiting for transfers between devices: 279 us -> none  [the longest x1 150 us: local(): lax.all_gather(rows_full, 'dp', axis=0, tiled=True)]
    pallas_call x0 -> x1, Pallas kernels: none -> 127 us  [local(): pl.pallas_call(kernel, out_shape=(jax.ShapeDtypeStruct((128, 5504), F32),...]
    dot_general x2 -> x0, matrix products: 19.5 us -> none  [the longest x1 12.8 us: local(): lax.dot_general(projected, out_grad, (((0,), (0,)), ((), ())), preferred_...]
  transfers between devices with their start and end apart: 3 -> 0, of which waited for: 3 -> 0; matrix products, arithmetic and copies ran while one was open for 0% -> 0% of each run, Pallas kernels for 0% -> 0%
where the time goes in v2:
time: 132 us
  Pallas kernels  127 us (96%)
  local copies, waits for them, and re-layouts  4.93 us (4%)
    pallas_call x1, Pallas kernels, local(): pl.pallas_call(kernel, out_shape=(jax.ShapeDtypeStruct((128, 5504), F32),...  127 us
    unnamed x7, local copies, waits for them, and re-layouts  4.93 us

profile of v2, /device:TPU:2, one launch (start us, length us, event | category | flops | bytes accessed | tf_op | source)
XLA Modules:
  0.0 132.3 jit_solution(11210228953199191290)
XLA Ops:
  0.6 126.7 %shard_map.85 = (f32[128,5504]{1,0:T(8,128)}, f32[8,5504]{1,0:T(8,128)}, f32[8,5504]{1,0:T(8,128)}) custom-call(bf16[256,8192]{1,0:T(8,128)(2,1)} %act_h.1, bf16[256,5504]{1,0:T(8,128)(2,1)} %og_h.1, bf16[128,128]{1,0:T(8,128)(2,1)} %bas_h.1, f32[128,5504]{1,0:T(8,128)} %mas_h.1, f32[8,5504]{1,0:T(8,128)} %fm_h.1, f32[8,5504]{1,0:T(8,128)} %sm_h.1), custom_call_target="tpu_custom_call" | custom-call | tf_op jit(solution)/shard_map/pallas_call | solution.py:390
  127.4 0.0 copy-start.1
  127.4 0.0 copy-start
  127.4 3.6 %copy.12 = f32[128,5504]{1,0:T(8,128)} copy(f32[128,5504]{1,0:T(8,128)} %get-tuple-element.6) | data formatting | bytes 5636096
  131.0 0.0 copy-done.1
  131.0 0.7 copy.13
  131.6 0.0 copy-done
  131.6 0.7 copy.14
Async XLA Ops:
  127.4 3.6 %copy-start.1 = (f32[8,5504]{1,0:T(8,128)S(1)}, f32[8,5504]{1,0:T(8,128)}, u32[]{:S(2)}) copy-start(f32[8,5504]{1,0:T(8,128)} %get-tuple-element.7) | copy-start | bytes 528388
  127.4 4.3 %copy-start = (f32[8,5504]{1,0:T(8,128)S(1)}, f32[8,5504]{1,0:T(8,128)}, u32[]{:S(2)}) copy-start(f32[8,5504]{1,0:T(8,128)} %get-tuple-element.8) | copy-start | bytes 528388

commit v3 on v2

--- a/solution.py
+++ b/solution.py
@@ -29,7 +29,7 @@
 def kernel(
     act_h, og_h, bas_h, mas_h, fm_h, sm_h,
     om, of, os_,
-    act, og, bas, mas, projt, part, rsr, mom, sec, nfr, nsr, fac, home, lhs, exs, exr,
+    act, og, bas, mas, projt, part, ra, rb, rc, rd, mom, sec, nfr, nsr, fac, home, lhs, exs, exr,
     lsem, bs, br, zs, zr, gs, gr, ms, mr, p1s, p1r, p2s, p2r, cs, cr,
     ts, tr, rs, rr, fs, fr, qs, qr, us, ur, es, er, ns, nr,
 ):
@@ -69,6 +69,7 @@
     t1 = t + 1 - 2 * lax.rem(t, 2)
     t2 = lax.rem(t + 2, 4)
     ring = ((dev(yh, wrapz(z + 1), x), t), (dev(yh, wrapz(z - 1), x), t))
+    far = ((dev(yh, wrapz(z + 2), x), t), (dev(yh, wrapz(z - 2), x), t))
     dy = dev(1 - yh, z, x)
     group = [None]
     for j in range(1, NG):
@@ -76,7 +77,7 @@
         group.append((dev(yy, z, xx), t))
     core = (d, t1)
     yside = ((d, t2), (dy, t2), (dy, t))
-    partners = group[1:] + [ring[0], ring[1], core, (d, t2), (dy, t2)]
+    partners = group[1:] + [ring[0], ring[1], far[0], far[1], core, (d, t2), (dy, t2)]
 
     eight = span(g * 8, 8)
     loads = [
@@ -189,6 +190,11 @@
     for i, rows in enumerate((low_t, low_u)):
         blk = projt.at[:, rows, cols_x]
         xb += [go(rcopy(blk, blk, p2s.at[4 * i + 3 + j], p2r.at[4 * i + 3 + j], group[j])) for j in (2, 1, 3)]
+    m_in = []
+    for j in ORDER:
+        cols = pl.ds(start_of(index(j, 1)), W)
+        m_in.append(go(rcopy(fm_h.at[:, cols], mom.at[eight], ms.at[0, j], mr.at[0, j], group[j])))
+        m_in.append(go(rcopy(sm_h.at[:, cols], sec.at[eight], ms.at[1, j], mr.at[1, j], group[j])))
     blk = projt.at[yh, top_t]
     c_in = [go(rcopy(blk, blk, cs.at[0], cr.at[0], core))]
     for i, (rows, yy) in enumerate([(top_u, yh), (top_u, 1 - yh), (top_t, 1 - yh)]):
@@ -208,41 +214,74 @@
 
     def multiply(c):
         cols = slice(c * CW, c * CW + CW)
-        part[:, cols] = jnp.dot(
+        total = jnp.dot(
             projt[0], og[0:4, :, cols].reshape(1024, CW), preferred_element_type=F32
         ) + jnp.dot(projt[1], og[4:8, :, cols].reshape(1024, CW), preferred_element_type=F32)
-
-    def rows_of(w, b):
-        return pl.ds(pl.multiple_of(w * 256 + b * 32, 32), 32)
-
-    def rsend(w, h, c, s):
-        b = wrapz(z + 4 - s) if w == 0 else wrapz(z - 4 + s)
-        src = part.at[rows_of(h, b), pl.ds(c * CW, CW)]
-        return go(rcopy(src, rsr.at[w, h, c, s], rs.at[w, h, c, s], rr.at[w, h, c, s], ring[w]))
-
-    moving = {}
+        part[:, :, cols] = total.reshape(2, 256, CW)
+
+    def rank_rows(w, away):
+        return span(wrapz(z + away if w == 0 else z - away) * 32, 32)
+
+    hop = {}
+
+    def leg(c, w, kind, src, dst, to):
+        hop[(c, w, kind)] = go(rcopy(src, dst.at[c, w], rs.at[c, w, kind], rr.at[c, w, kind], to[w]))
 
     def begin(c):
         multiply(c)
-        for w, h in ((0, 0), (1, 1), (0, 1), (1, 0)):
-            moving[(w, h, c)] = rsend(w, h, c, 0 if w == h else 1)
-
-    def reduce(c, s):
-        for w, h in ((0, 0), (1, 1), (0, 1), (1, 0)):
-            if s == 0 and w != h:
-                continue
-            moving[(w, h, c)].wait_recv()
-            b = wrapz(z + 3 - s) if w == 0 else wrapz(z - 3 + s)
-            cols = pl.ds(c * CW, CW)
-            part[rows_of(h, b), cols] = part[rows_of(h, b), cols] + rsr[w, h, c, s]
-            if s < 3:
-                moving[(w, h, c)] = rsend(w, h, c, s + 1)
+        cols = pl.ds(c * CW, CW)
+        for w in (0, 1):
+            leg(c, w, 0, part.at[:, rank_rows(w, 3), cols], ra, ring)
+            leg(c, w, 1, part.at[w, rank_rows(w, 4), cols], rb, far)
+        for w in (0, 1):
+            leg(c, w, 2, part.at[:, rank_rows(w, 1), cols], rc, ring)
+
+    def middle(c):
+        cols = pl.ds(c * CW, CW)
+        for w in (0, 1):
+            rows = rank_rows(w, 2)
+            hop[(c, w, 0)].wait_recv()
+            part[:, rows, cols] = part[:, rows, cols] + ra[c, w]
+            hop[(c, w, 1)].wait_recv()
+            part[w, rows, cols] = part[w, rows, cols] + rb[c, w]
+            leg(c, w, 3, part.at[:, rows, cols], rd, far)
+
+    def close(c):
+        cols = pl.ds(c * CW, CW)
+        rows = rank_rows(0, 0)
+        for w in (0, 1):
+            hop[(c, w, 2)].wait_recv()
+            hop[(c, w, 3)].wait_recv()
+            part[:, rows, cols] = part[:, rows, cols] + (rc[c, w] + rd[c, w])
+
+    def fleg(c, w, kind, blk, to):
+        hop[(c, w, 4 + kind)] = go(
+            rcopy(blk, blk, fs.at[c - 1, w, kind], fr.at[c - 1, w, kind], to[w])
+        )
+
+    def spread(c):
+        for w in (0, 1):
+            fleg(c, w, 1, fac.at[c - 1, :, z], far)
+        for w in (0, 1):
+            fleg(c, w, 0, fac.at[c - 1, :, z], ring)
+
+    def forward(c):
+        for w in (0, 1):
+            hop[(c, w, 5)].wait_recv()
+            zz = wrapz(z - 2) if w == 0 else wrapz(z + 2)
+            fleg(c, w, 3, fac.at[c - 1, w, zz], far)
+            fleg(c, w, 2, fac.at[c - 1, :, zz], ring)
+
+    def gathered(c):
+        for w in (0, 1):
+            for kind in (0, 2, 3):
+                hop[(c, w, 4 + kind)].wait_recv()
 
     def adam(c, put):
         cols = slice(c * CW, c * CW + CW)
         for w in (0, 1):
             rows = slice(w * 32, w * 32 + 32)
-            grad = part[rows_of(w, z), cols]
+            grad = part[w, rank_rows(0, 0), cols]
             first = decay_first * mom[rows, cols] + (1.0 - decay_first) * grad
             second = decay_second * sec[rows, cols] + (1.0 - decay_second) * grad * grad
             mom[rows, cols] = first
@@ -260,41 +299,30 @@
 
     begin(1)
     begin(0)
-    m_in = []
-    for j in ORDER:
-        cols = pl.ds(start_of(index(j, 1)), W)
-        m_in.append(go(rcopy(fm_h.at[:, cols], mom.at[eight], ms.at[0, j], mr.at[0, j], group[j])))
-        m_in.append(go(rcopy(sm_h.at[:, cols], sec.at[eight], ms.at[1, j], mr.at[1, j], group[j])))
     g_in.append(grad_send(1, 512, 256))
     t_in.append(go(rcopy(bas.at[z], lhs.at[:, :, rows_t], ts.at[1], tr.at[1], (d, t2))))
-    for s in range(4):
-        reduce(1, s)
-        reduce(0, s)
+    middle(1)
+    middle(0)
+    close(1)
     loads[4].wait()
     loads[5].wait()
     for c in m_in:
         c.wait_recv()
-    step1, last1 = gather(lambda zz, h: fac.at[0, h, zz], fs.at[0], fr.at[0])
-    step2, last2 = gather(lambda zz, h: fac.at[1, h, zz], fs.at[1], fr.at[1])
     step0, last0 = gather(lambda zz, h: home.at[:, h, zz], us, ur)
     adam(1, put_fac(1))
-    step1(0)
+    spread(1)
+    close(0)
     adam(0, put_home)
     blk = home.at[g, :, z]
     q_in = [go(rcopy(blk, blk, qs.at[j], qr.at[j], group[j])) for j in ORDER]
+    forward(1)
     for c in g_in[1]:
         c.wait_recv()
     begin(2)
-    step1(1)
-    reduce(2, 0)
-    step1(2)
-    reduce(2, 1)
-    step1(3)
-    reduce(2, 2)
     t_in[1].wait_recv()
     blk = lhs.at[:, :, rows_u]
     t_in.append(go(rcopy(blk, blk, ts.at[2], tr.at[2], core)))
-    last1()
+    gathered(1)
 
     e_in = {}
 
@@ -320,12 +348,15 @@
         if c is not t_in[1]:
             c.wait_recv()
     expand(1)
-    reduce(2, 3)
+    middle(2)
+    close(2)
     adam(2, put_fac(2))
-    step2(0)
+    spread(2)
     for c in q_in:
         c.wait_recv()
     step0(0)
+    forward(2)
+    step0(1)
     n_in = []
     for j in ORDER:
         rows = span(index(j, 1) * 8, 8)
@@ -333,12 +364,9 @@
         n_in.append(go(rcopy(sec.at[rows], nsr.at[g], ns.at[1, j], nr.at[1, j], group[j])))
     nfr[g] = mom[eight]
     nsr[g] = sec[eight]
-    step2(1)
-    step2(2)
-    step2(3)
-    step0(1)
-    last2()
+    gathered(2)
     expand(2)
+    step0(2)
     for c in n_in:
         c.wait_recv()
     for k in range(NG):
@@ -346,7 +374,6 @@
         of[:, at : at + W] = nfr[k]
         os_[:, at : at + W] = nsr[k]
     loads[2].wait()
-    step0(2)
     step0(3)
     last0()
     for k in range(NG):
@@ -379,8 +406,8 @@
         (12,),
         (6,),
         (3,),
-        (2, 2, NC, 4),
-        (2, 2, 4, 2),
+        (NC, 2, 4),
+        (2, 2, 4),
         (8,),
         (2, 4, 2),
         (2, 8),
@@ -402,8 +429,11 @@
             pltpu.VMEM((NZ, NG, 128, 128), BF16),
             pltpu.VMEM((128, 5504), F32),
             pltpu.VMEM((2, 512, 1024), BF16),
-            pltpu.VMEM((512, W), F32),
-            pltpu.VMEM((2, 2, NC, 4, 32, CW), F32),
+            pltpu.VMEM((2, 256, W), F32),
+            pltpu.VMEM((NC, 2, 2, 32, CW), F32),
+            pltpu.VMEM((NC, 2, 32, CW), F32),
+            pltpu.VMEM((NC, 2, 2, 32, CW), F32),
+            pltpu.VMEM((NC, 2, 2, 32, CW), F32),
             pltpu.VMEM((64, W), F32),
             pltpu.VMEM((64, W), F32),
             pltpu.VMEM((NG, 8, W), F32),

time: 132 us -> 126 us (0.955); the launches traced: 132 us -> 124 us
  Pallas kernels: 127 us -> 118 us
    pallas_call x1, Pallas kernels: 127 us -> 118 us  [local(): pl.pallas_call(kernel, out_shape=(jax.ShapeDtypeStruct((128, 5504), F32),...]
where the time goes in v3:
time: 126 us; the launch traced here: 124 us
  Pallas kernels  118 us (94%)
  local copies, waits for them, and re-layouts  4.93 us (4%)
    pallas_call x1, Pallas kernels, local(): pl.pallas_call(kernel, out_shape=(jax.ShapeDtypeStruct((128, 5504), F32),...  118 us
    unnamed x7, local copies, waits for them, and re-layouts  4.93 us

profile of v3, /device:TPU:2, one launch (start us, length us, event | category | flops | bytes accessed | tf_op | source)
XLA Modules:
  0.0 124.1 jit_solution(4251948757138460403)
XLA Ops:
  0.6 118.5 %shard_map.85 = (f32[128,5504]{1,0:T(8,128)}, f32[8,5504]{1,0:T(8,128)}, f32[8,5504]{1,0:T(8,128)}) custom-call(bf16[256,8192]{1,0:T(8,128)(2,1)} %act_h.1, bf16[256,5504]{1,0:T(8,128)(2,1)} %og_h.1, bf16[128,128]{1,0:T(8,128)(2,1)} %bas_h.1, f32[128,5504]{1,0:T(8,128)} %mas_h.1, f32[8,5504]{1,0:T(8,128)} %fm_h.1, f32[8,5504]{1,0:T(8,128)} %sm_h.1), custom_call_target="tpu_custom_call" | custom-call | tf_op jit(solution)/shard_map/pallas_call | solution.py:417
  119.1 0.0 copy-start.1
  119.1 0.0 copy-start
  119.1 3.6 %copy.12 = f32[128,5504]{1,0:T(8,128)} copy(f32[128,5504]{1,0:T(8,128)} %get-tuple-element.6) | data formatting | bytes 5636096
  122.7 0.0 copy-done.1
  122.7 0.7 copy.13
  123.4 0.0 copy-done
  123.4 0.7 copy.14
Async XLA Ops:
  119.1 3.6 %copy-start.1 = (f32[8,5504]{1,0:T(8,128)S(1)}, f32[8,5504]{1,0:T(8,128)}, u32[]{:S(2)}) copy-start(f32[8,5504]{1,0:T(8,128)} %get-tuple-element.7) | copy-start | bytes 528388
  119.1 4.3 %copy-start = (f32[8,5504]{1,0:T(8,128)S(1)}, f32[8,5504]{1,0:T(8,128)}, u32[]{:S(2)}) copy-start(f32[8,5504]{1,0:T(8,128)} %get-tuple-element.8) | copy-start | bytes 528388

commit v4 on v3

--- a/solution.py
+++ b/solution.py
@@ -367,14 +367,14 @@
     gathered(2)
     expand(2)
     step0(2)
+    loads[2].wait()
+    step0(3)
     for c in n_in:
         c.wait_recv()
     for k in range(NG):
         at = min(k * (W // 128), TOP) * 128
         of[:, at : at + W] = nfr[k]
         os_[:, at : at + W] = nsr[k]
-    loads[2].wait()
-    step0(3)
     last0()
     for k in range(NG):
         at = min(k * (W // 128), TOP) * 128
@@ -392,6 +392,24 @@
         finish(index(j, -1))
     for c in sends:
         c.wait_send()
+
+
+PIECES = 8
+
+
+def write(om_h, of_h, os_h, om, of, os_, big, first, second, sem):
+    rows = om_h.shape[0] // PIECES
+    cut = [pl.ds(i * rows, rows) for i in range(PIECES)]
+    legs = [(om_h.at[c], big.at[c], om.at[c]) for c in cut] + [(of_h, first, of), (os_h, second, os_)]
+    loads = [pltpu.make_async_copy(a, b, sem.at[0, i]) for i, (a, b, _) in enumerate(legs)]
+    stores = [pltpu.make_async_copy(b, c, sem.at[1, i]) for i, (_, b, c) in enumerate(legs)]
+    for c in loads:
+        c.start()
+    for c, e in zip(loads, stores):
+        c.wait()
+        e.start()
+    for e in stores:
+        e.wait()
 
 
 def local(activations, out_grad, basis, master, first_moment, second_moment):
@@ -414,7 +432,7 @@
         (2, 8),
     ):
         sems += [dma(shape), dma(shape)]
-    return pl.pallas_call(
+    results = pl.pallas_call(
         kernel,
         out_shape=(
             jax.ShapeDtypeStruct((128, 5504), F32),
@@ -449,6 +467,13 @@
             collective_id=0, has_side_effects=True, vmem_limit_bytes=56 << 20
         ),
     )(activations, out_grad, basis, master, first_moment, second_moment)
+    return pl.pallas_call(
+        write,
+        out_shape=tuple(jax.ShapeDtypeStruct(r.shape, r.dtype) for r in results),
+        in_specs=[pl.BlockSpec(memory_space=pl.ANY)] * 3,
+        out_specs=[pl.BlockSpec(memory_space=pl.ANY)] * 3,
+        scratch_shapes=[pltpu.VMEM(r.shape, r.dtype) for r in results] + [dma((2, PIECES + 2))],
+    )(*results)
 
 
 def solution(mesh):

time: 126 us -> 122 us (0.968); the launches traced: 124 us -> 122 us
  local copies, waits for them, and re-layouts: 4.93 us -> 0 us
  Pallas kernels: 118 us -> 121 us
    unnamed x7 -> x0, local copies, waits for them, and re-layouts: 4.93 us -> none
    pallas_call x0 -> x1, Pallas kernels: none -> 2.82 us  [local(): pl.pallas_call(write, out_shape=tuple((jax.ShapeDtypeStruct(r.shape, r.dt...]
where the time goes in v4:
time: 122 us
  Pallas kernels  121 us (99%)
    pallas_call x1, Pallas kernels, local(): pl.pallas_call(kernel, out_shape=(jax.ShapeDtypeStruct((128, 5504), F32),...  118 us
    pallas_call x1, Pallas kernels, local(): pl.pallas_call(write, out_shape=tuple((jax.ShapeDtypeStruct(r.shape, r.dt...  2.82 us

profile of v4, /device:TPU:2, one launch (start us, length us, event | category | flops | bytes accessed | tf_op | source)
XLA Modules:
  0.0 121.9 jit_solution(6148716924546377775)
XLA Ops:
  0.6 118.5 %shard_map.85 = (f32[128,5504]{1,0:T(8,128)}, f32[8,5504]{1,0:T(8,128)}, f32[8,5504]{1,0:T(8,128)}) custom-call(bf16[256,8192]{1,0:T(8,128)(2,1)} %act_h.1, bf16[256,5504]{1,0:T(8,128)(2,1)} %og_h.1, bf16[128,128]{1,0:T(8,128)(2,1)} %bas_h.1, f32[128,5504]{1,0:T(8,128)} %mas_h.1, f32[8,5504]{1,0:T(8,128)} %fm_h.1, f32[8,5504]{1,0:T(8,128)} %sm_h.1), custom_call_target="tpu_custom_call" | custom-call | tf_op jit(solution)/shard_map/pallas_call | solution.py:435
  119.1 2.8 %shard_map.86 = (f32[128,5504]{1,0:T(8,128)}, f32[8,5504]{1,0:T(8,128)}, f32[8,5504]{1,0:T(8,128)}) custom-call(f32[128,5504]{1,0:T(8,128)} %get-tuple-element.6.om_h, f32[8,5504]{1,0:T(8,128)} %get-tuple-element.7.of_h, f32[8,5504]{1,0:T(8,128)} %get-tuple-element.8.os_h), custom_call_target="tpu_custom_call" | custom-call | tf_op jit(solution)/shard_map/pallas_call | solution.py:470

commit v5 on v4

--- a/solution.py
+++ b/solution.py
@@ -347,16 +347,11 @@
     for c in t_in:
         if c is not t_in[1]:
             c.wait_recv()
+    middle(2)
     expand(1)
-    middle(2)
     close(2)
     adam(2, put_fac(2))
     spread(2)
-    for c in q_in:
-        c.wait_recv()
-    step0(0)
-    forward(2)
-    step0(1)
     n_in = []
     for j in ORDER:
         rows = span(index(j, 1) * 8, 8)
@@ -364,6 +359,11 @@
         n_in.append(go(rcopy(sec.at[rows], nsr.at[g], ns.at[1, j], nr.at[1, j], group[j])))
     nfr[g] = mom[eight]
     nsr[g] = sec[eight]
+    for c in q_in:
+        c.wait_recv()
+    step0(0)
+    forward(2)
+    step0(1)
     gathered(2)
     expand(2)
     step0(2)

time: 122 us -> 122 us (level); the launches traced: 122 us -> 120 us
    pallas_call x1, Pallas kernels: 118 us -> 117 us  [local(): pl.pallas_call(kernel, out_shape=(jax.ShapeDtypeStruct((128, 5504), F32),...]
where the time goes in v5:
time: 122 us; the launch traced here: 120 us
  Pallas kernels  120 us (98%)
    pallas_call x1, Pallas kernels, local(): pl.pallas_call(kernel, out_shape=(jax.ShapeDtypeStruct((128, 5504), F32),...  117 us
    pallas_call x1, Pallas kernels, local(): pl.pallas_call(write, out_shape=tuple((jax.ShapeDtypeStruct(r.shape, r.dt...  2.82 us

profile of v5, /device:TPU:2, one launch (start us, length us, event | category | flops | bytes accessed | tf_op | source)
XLA Modules:
  0.0 120.3 jit_solution(6692843566039405969)
XLA Ops:
  0.6 116.8 %shard_map.85 = (f32[128,5504]{1,0:T(8,128)}, f32[8,5504]{1,0:T(8,128)}, f32[8,5504]{1,0:T(8,128)}) custom-call(bf16[256,8192]{1,0:T(8,128)(2,1)} %act_h.1, bf16[256,5504]{1,0:T(8,128)(2,1)} %og_h.1, bf16[128,128]{1,0:T(8,128)(2,1)} %bas_h.1, f32[128,5504]{1,0:T(8,128)} %mas_h.1, f32[8,5504]{1,0:T(8,128)} %fm_h.1, f32[8,5504]{1,0:T(8,128)} %sm_h.1), custom_call_target="tpu_custom_call" | custom-call | tf_op jit(solution)/shard_map/pallas_call | solution.py:435
  117.5 2.8 %shard_map.86 = (f32[128,5504]{1,0:T(8,128)}, f32[8,5504]{1,0:T(8,128)}, f32[8,5504]{1,0:T(8,128)}) custom-call(f32[128,5504]{1,0:T(8,128)} %get-tuple-element.6.om_h, f32[8,5504]{1,0:T(8,128)} %get-tuple-element.7.of_h, f32[8,5504]{1,0:T(8,128)} %get-tuple-element.8.os_h), custom_call_target="tpu_custom_call" | custom-call | tf_op jit(solution)/shard_map/pallas_call | solution.py:470
